TPU v7x, 32 devices: a whole 2x2x4 slice. The times are simulated.
32 devices in a mesh: grp: 8 (over y, x, core), seq: 4 (over z).
Axes of the slice: x: 2, y: 2, z: 4, core: 2. Of those that a mesh axis runs over, the one named last changes fastest.
Arguments:
- tokens: bfloat16 [32, 512, 1024], P('grp', 'seq'), may hold values from -6 to 6
- segment_ids: int32 [32, 512], P('grp'), may hold values from 0 to 17, as said below
- w_query: bfloat16 [1024, 1024], P(('grp', 'seq')), may hold values from -0.375 to 0.375
- w_key: bfloat16 [1024, 1024], P(('grp', 'seq')), may hold values from -0.1875 to 0.1875
- w_value: bfloat16 [1024, 1024], P(('grp', 'seq')), may hold values from -0.1875 to 0.1875
- w_output: bfloat16 [1024, 1024], P(('grp', 'seq')), may hold values from -0.5 to 0.5
- w_inner: bfloat16 [1024, 4096], P(('grp', 'seq')), may hold values from -0.1875 to 0.1875
- w_outer: bfloat16 [4096, 1024], P(('grp', 'seq')), may hold values from -0.125 to 0.125
- b_query: bfloat16 [1024], P(('grp', 'seq')), may hold values from -3 to 3
- b_value: bfloat16 [1024], P(('grp', 'seq')), may hold values from -3 to 3
- b_output: bfloat16 [1024], P(('grp', 'seq')), may hold values from -3 to 3
- b_inner: bfloat16 [4096], P(('grp', 'seq')), may hold values from -3 to 3
- b_outer: bfloat16 [1024], P(('grp', 'seq')), may hold values from -3 to 3
- norm1_gain: bfloat16 [1024], P(('grp', 'seq')), may hold values from 0.099609375 to 1.8984375
- norm1_bias: bfloat16 [1024], P(('grp', 'seq')), may hold values from -3 to 3
- norm2_gain: bfloat16 [1024], P(('grp', 'seq')), may hold values from 0.099609375 to 1.8984375
- norm2_bias: bfloat16 [1024], P(('grp', 'seq')), may hold values from -3 to 3
- cotangent: bfloat16 [32, 512, 1024], P('grp', 'seq'), may hold values from -6 to 6
Outputs:
- layer_out: bfloat16 [32, 512, 1024], P('grp', 'seq')
- grad_tokens: bfloat16 [32, 512, 1024], P('grp', 'seq')
- grad_w_query: float32 [1024, 1024], P('grp')
- grad_w_key: float32 [1024, 1024], P('grp')
- grad_w_value: float32 [1024, 1024], P('grp')
- grad_w_output: float32 [1024, 1024], P('grp')
- grad_w_inner: float32 [1024, 4096], P('grp')
- grad_w_outer: float32 [4096, 1024], P('grp')
- grad_b_query: float32 [1024], P('grp')
- grad_b_value: float32 [1024], P('grp')
- grad_b_output: float32 [1024], P('grp')
- grad_b_inner: float32 [4096], P('grp')
- grad_b_outer: float32 [1024], P('grp')
- grad_norm1_gain: float32 [1024], P('grp')
- grad_norm1_bias: float32 [1024], P('grp')
- grad_norm2_gain: float32 [1024], P('grp')
- grad_norm2_bias: float32 [1024], P('grp')
Inputs may be any that keep to these rules, and one draw needn't show every extreme that they name: `segment_ids`: within a sequence equal nonzero ids form one run of positions (a document), ids never fall except to 0, and 0 marks padding at the sequence's end.
All inputs are finite; a program needn't handle non-finite values.
Results may differ from a plain program's by a relative error of at most 0.02.
Values may be sent and summed in bfloat16 or wider, within the bound.
A program may use at most 192 MiB of HBM per device.

v0:
```python
import math

import jax
import jax.numpy as jnp
from jax import lax
from jax.sharding import PartitionSpec as P

H = 16
HD = 64


def normalize(row_data, gain_row, shift_row):
    centered = row_data - jnp.mean(row_data, axis=-1, keepdims=True)
    variance = jnp.mean(centered * centered, axis=-1, keepdims=True)
    return centered * lax.rsqrt(variance + 1e-06) * gain_row + shift_row


def exact_gelu(values_in):
    return jax.nn.gelu(values_in, approximate=False)


def project(left, right):
    return jnp.einsum("scd,de->sce", left, right, preferred_element_type=jnp.float32)


def weight_grad(left, right):
    return jnp.einsum("scd,sce->de", left, right, preferred_element_type=jnp.float32)


def back_project(grad_in, right):
    return jnp.einsum("sce,de->scd", grad_in, right, preferred_element_type=jnp.float32)


def column_sum(grad_in):
    return jnp.sum(grad_in.astype(jnp.float32), axis=(0, 1))


def head_split(block_rows):
    return block_rows.reshape(block_rows.shape[0], H, HD)


def scores_of(query_rows, key_rows, allowed):
    raw = jnp.einsum(
        "chd,khd->hck",
        head_split(query_rows),
        head_split(key_rows),
        preferred_element_type=jnp.float32,
    ) * (1.0 / math.sqrt(HD))
    return jnp.where(allowed[None], raw, -1e30)


def forward_one(pieces):
    query_rows, key_rows, value_rows, allowed = pieces
    scores = scores_of(query_rows, key_rows, allowed)
    top = jnp.max(scores, axis=-1, keepdims=True)
    expo = jnp.exp(scores - top)
    total = jnp.sum(expo, axis=-1, keepdims=True)
    probs = (expo / total).astype(jnp.bfloat16)
    mixed = jnp.einsum(
        "hck,khd->chd", probs, head_split(value_rows), preferred_element_type=jnp.float32
    )
    return (mixed.reshape(query_rows.shape).astype(jnp.bfloat16), top + jnp.log(total))


def backward_one(pieces):
    query_rows, key_rows, value_rows, allowed, log_total, grad_rows = pieces
    scale_factor = 1.0 / math.sqrt(HD)
    scores = scores_of(query_rows, key_rows, allowed)
    probs = jnp.exp(scores - log_total)
    grad_heads = head_split(grad_rows)
    grad_probs = jnp.einsum(
        "chd,khd->hck", grad_heads, head_split(value_rows), preferred_element_type=jnp.float32
    )
    grad_scores = probs * (grad_probs - jnp.sum(probs * grad_probs, axis=-1, keepdims=True))
    grad_scores = grad_scores.astype(jnp.bfloat16)
    grad_query = (
        jnp.einsum(
            "hck,khd->chd", grad_scores, head_split(key_rows), preferred_element_type=jnp.float32
        )
        * scale_factor
    )
    grad_key = (
        jnp.einsum(
            "hck,chd->khd", grad_scores, head_split(query_rows), preferred_element_type=jnp.float32
        )
        * scale_factor
    )
    grad_value = jnp.einsum(
        "hck,chd->khd", probs.astype(jnp.bfloat16), grad_heads, preferred_element_type=jnp.float32
    )
    return (
        grad_query.reshape(query_rows.shape).astype(jnp.bfloat16),
        grad_key.reshape(key_rows.shape),
        grad_value.reshape(key_rows.shape),
    )


def local(
    tokens,
    segment_ids,
    w_query,
    w_key,
    w_value,
    w_output,
    w_inner,
    w_outer,
    b_query,
    b_value,
    b_output,
    b_inner,
    b_outer,
    norm1_gain,
    norm1_bias,
    norm2_gain,
    norm2_bias,
    cotangent,
):
    shards = (
        w_query,
        w_key,
        w_value,
        w_output,
        w_inner,
        w_outer,
        b_query,
        b_value,
        b_output,
        b_inner,
        b_outer,
        norm1_gain,
        norm1_bias,
        norm2_gain,
        norm2_bias,
    )
    gathered = (
        lax.all_gather(shards[0], ("grp", "seq"), axis=0, tiled=True),
        lax.all_gather(shards[1], ("grp", "seq"), axis=0, tiled=True),
        lax.all_gather(shards[2], ("grp", "seq"), axis=0, tiled=True),
        lax.all_gather(shards[3], ("grp", "seq"), axis=0, tiled=True),
        lax.all_gather(shards[4], ("grp", "seq"), axis=0, tiled=True),
        lax.all_gather(shards[5], ("grp", "seq"), axis=0, tiled=True),
        lax.all_gather(shards[6], ("grp", "seq"), axis=0, tiled=True),
        lax.all_gather(shards[7], ("grp", "seq"), axis=0, tiled=True),
        lax.all_gather(shards[8], ("grp", "seq"), axis=0, tiled=True),
        lax.all_gather(shards[9], ("grp", "seq"), axis=0, tiled=True),
        lax.all_gather(shards[10], ("grp", "seq"), axis=0, tiled=True),
        lax.all_gather(shards[11], ("grp", "seq"), axis=0, tiled=True),
        lax.all_gather(shards[12], ("grp", "seq"), axis=0, tiled=True),
        lax.all_gather(shards[13], ("grp", "seq"), axis=0, tiled=True),
        lax.all_gather(shards[14], ("grp", "seq"), axis=0, tiled=True),
    )
    (
        wide_query,
        wide_key,
        wide_value,
        wide_output,
        wide_inner,
        wide_outer,
        bias_query,
        bias_value,
        bias_output,
        bias_inner,
        bias_outer,
        gain_first,
        shift_first,
        gain_second,
        shift_second,
    ) = gathered
    rows_tokens, rows_seed = (tokens, cotangent)
    block_len = tokens.shape[1]
    offset = lax.axis_index("seq") * block_len
    query_labels = lax.dynamic_slice_in_dim(segment_ids, offset, block_len, 1)
    queries = (project(rows_tokens, wide_query) + bias_query).astype(jnp.bfloat16)
    own_keys = project(rows_tokens, wide_key).astype(jnp.bfloat16)
    own_values = (project(rows_tokens, wide_value) + bias_value).astype(jnp.bfloat16)
    all_keys, all_values = (
        lax.all_gather(own_keys, "seq", axis=1, tiled=True),
        lax.all_gather(own_values, "seq", axis=1, tiled=True),
    )
    places = jnp.arange(segment_ids.shape[1])
    query_places = offset + jnp.arange(block_len)
    allowed = (query_labels[:, :, None] == segment_ids[:, None, :]) & (
        segment_ids[:, None, :] != 0
    ) | (query_places[None, :, None] == places[None, None, :])
    context, log_total = lax.map(forward_one, (queries, all_keys, all_values, allowed))
    attention = project(context, wide_output) + bias_output
    first, first_pull = jax.vjp(
        normalize,
        rows_tokens.astype(jnp.float32) + attention,
        gain_first.astype(jnp.float32),
        shift_first.astype(jnp.float32),
    )
    first_low = first.astype(jnp.bfloat16)
    inner = project(first_low, wide_inner) + bias_inner
    hidden_full, gelu_pull = jax.vjp(exact_gelu, inner)
    hidden = hidden_full.astype(jnp.bfloat16)
    outer = project(hidden, wide_outer) + bias_outer
    second, second_pull = jax.vjp(
        normalize, first + outer, gain_second.astype(jnp.float32), shift_second.astype(jnp.float32)
    )
    layer_rows = second.astype(jnp.bfloat16)
    again = (
        lax.all_gather(shards[0], ("grp", "seq"), axis=0, tiled=True),
        lax.all_gather(shards[1], ("grp", "seq"), axis=0, tiled=True),
        lax.all_gather(shards[2], ("grp", "seq"), axis=0, tiled=True),
        lax.all_gather(shards[3], ("grp", "seq"), axis=0, tiled=True),
        lax.all_gather(shards[4], ("grp", "seq"), axis=0, tiled=True),
        lax.all_gather(shards[5], ("grp", "seq"), axis=0, tiled=True),
        lax.all_gather(shards[6], ("grp", "seq"), axis=0, tiled=True),
        lax.all_gather(shards[7], ("grp", "seq"), axis=0, tiled=True),
        lax.all_gather(shards[8], ("grp", "seq"), axis=0, tiled=True),
        lax.all_gather(shards[9], ("grp", "seq"), axis=0, tiled=True),
        lax.all_gather(shards[10], ("grp", "seq"), axis=0, tiled=True),
        lax.all_gather(shards[11], ("grp", "seq"), axis=0, tiled=True),
        lax.all_gather(shards[12], ("grp", "seq"), axis=0, tiled=True),
        lax.all_gather(shards[13], ("grp", "seq"), axis=0, tiled=True),
        lax.all_gather(shards[14], ("grp", "seq"), axis=0, tiled=True),
    )
    back_query, back_key, back_value, back_output, back_inner, back_outer = (
        again[0],
        again[1],
        again[2],
        again[3],
        again[4],
        again[5],
    )
    grad_second, grad_gain_second, grad_shift_second = second_pull(rows_seed.astype(jnp.float32))
    grad_outer = grad_second.astype(jnp.bfloat16)
    (grad_inner_full,) = gelu_pull(back_project(grad_outer, back_outer))
    grad_inner = grad_inner_full.astype(jnp.bfloat16)
    grad_first = grad_second + back_project(grad_inner, back_inner)
    grad_resid, grad_gain_first, grad_shift_first = first_pull(grad_first)
    grad_attention = grad_resid.astype(jnp.bfloat16)
    grad_context = back_project(grad_attention, back_output).astype(jnp.bfloat16)
    grad_queries, key_terms, value_terms = lax.map(
        backward_one, (queries, all_keys, all_values, allowed, log_total, grad_context)
    )
    key_sums, value_sums = (
        lax.psum_scatter(
            key_terms.astype(jnp.bfloat16), "seq", scatter_dimension=1, tiled=True
        ).astype(jnp.float32),
        lax.psum_scatter(
            value_terms.astype(jnp.bfloat16), "seq", scatter_dimension=1, tiled=True
        ).astype(jnp.float32),
    )
    grad_keys = key_sums.astype(jnp.bfloat16)
    grad_values = value_sums.astype(jnp.bfloat16)
    grad_rows = (
        grad_resid
        + back_project(grad_queries, back_query)
        + back_project(grad_keys, back_key)
        + back_project(grad_values, back_value)
    ).astype(jnp.bfloat16)
    layer_out, grad_tokens = (layer_rows, grad_rows)
    gradients = (
        weight_grad(rows_tokens, grad_queries),
        weight_grad(rows_tokens, grad_keys),
        weight_grad(rows_tokens, grad_values),
        weight_grad(context, grad_attention),
        weight_grad(first_low, grad_inner),
        weight_grad(hidden, grad_outer),
        column_sum(grad_queries),
        column_sum(grad_values),
        column_sum(grad_attention),
        column_sum(grad_inner),
        column_sum(grad_outer),
        grad_gain_first,
        grad_shift_first,
        grad_gain_second,
        grad_shift_second,
    )
    partial_rows = (
        lax.psum_scatter(
            gradients[0].astype(jnp.bfloat16), "grp", scatter_dimension=0, tiled=True
        ).astype(jnp.float32),
        lax.psum_scatter(
            gradients[1].astype(jnp.bfloat16), "grp", scatter_dimension=0, tiled=True
        ).astype(jnp.float32),
        lax.psum_scatter(
            gradients[2].astype(jnp.bfloat16), "grp", scatter_dimension=0, tiled=True
        ).astype(jnp.float32),
        lax.psum_scatter(
            gradients[3].astype(jnp.bfloat16), "grp", scatter_dimension=0, tiled=True
        ).astype(jnp.float32),
        lax.psum_scatter(
            gradients[4].astype(jnp.bfloat16), "grp", scatter_dimension=0, tiled=True
        ).astype(jnp.float32),
        lax.psum_scatter(
            gradients[5].astype(jnp.bfloat16), "grp", scatter_dimension=0, tiled=True
        ).astype(jnp.float32),
        lax.psum_scatter(
            gradients[6].astype(jnp.bfloat16), "grp", scatter_dimension=0, tiled=True
        ).astype(jnp.float32),
        lax.psum_scatter(
            gradients[7].astype(jnp.bfloat16), "grp", scatter_dimension=0, tiled=True
        ).astype(jnp.float32),
        lax.psum_scatter(
            gradients[8].astype(jnp.bfloat16), "grp", scatter_dimension=0, tiled=True
        ).astype(jnp.float32),
        lax.psum_scatter(
            gradients[9].astype(jnp.bfloat16), "grp", scatter_dimension=0, tiled=True
        ).astype(jnp.float32),
        lax.psum_scatter(
            gradients[10].astype(jnp.bfloat16), "grp", scatter_dimension=0, tiled=True
        ).astype(jnp.float32),
        lax.psum_scatter(
            gradients[11].astype(jnp.bfloat16), "grp", scatter_dimension=0, tiled=True
        ).astype(jnp.float32),
        lax.psum_scatter(
            gradients[12].astype(jnp.bfloat16), "grp", scatter_dimension=0, tiled=True
        ).astype(jnp.float32),
        lax.psum_scatter(
            gradients[13].astype(jnp.bfloat16), "grp", scatter_dimension=0, tiled=True
        ).astype(jnp.float32),
        lax.psum_scatter(
            gradients[14].astype(jnp.bfloat16), "grp", scatter_dimension=0, tiled=True
        ).astype(jnp.float32),
    )
    summed = (
        lax.psum(partial_rows[0].astype(jnp.bfloat16), "seq").astype(jnp.float32),
        lax.psum(partial_rows[1].astype(jnp.bfloat16), "seq").astype(jnp.float32),
        lax.psum(partial_rows[2].astype(jnp.bfloat16), "seq").astype(jnp.float32),
        lax.psum(partial_rows[3].astype(jnp.bfloat16), "seq").astype(jnp.float32),
        lax.psum(partial_rows[4].astype(jnp.bfloat16), "seq").astype(jnp.float32),
        lax.psum(partial_rows[5].astype(jnp.bfloat16), "seq").astype(jnp.float32),
        lax.psum(partial_rows[6].astype(jnp.bfloat16), "seq").astype(jnp.float32),
        lax.psum(partial_rows[7].astype(jnp.bfloat16), "seq").astype(jnp.float32),
        lax.psum(partial_rows[8].astype(jnp.bfloat16), "seq").astype(jnp.float32),
        lax.psum(partial_rows[9].astype(jnp.bfloat16), "seq").astype(jnp.float32),
        lax.psum(partial_rows[10].astype(jnp.bfloat16), "seq").astype(jnp.float32),
        lax.psum(partial_rows[11].astype(jnp.bfloat16), "seq").astype(jnp.float32),
        lax.psum(partial_rows[12].astype(jnp.bfloat16), "seq").astype(jnp.float32),
        lax.psum(partial_rows[13].astype(jnp.bfloat16), "seq").astype(jnp.float32),
        lax.psum(partial_rows[14].astype(jnp.bfloat16), "seq").astype(jnp.float32),
    )
    return (
        layer_out,
        grad_tokens,
        summed[0],
        summed[1],
        summed[2],
        summed[3],
        summed[4],
        summed[5],
        summed[6],
        summed[7],
        summed[8],
        summed[9],
        summed[10],
        summed[11],
        summed[12],
        summed[13],
        summed[14],
    )


def solution(mesh):
    return jax.shard_map(
        local,
        mesh=mesh,
        in_specs=(
            P("grp", "seq", None),
            P("grp", None),
            P(("grp", "seq"), None),
            P(("grp", "seq"), None),
            P(("grp", "seq"), None),
            P(("grp", "seq"), None),
            P(("grp", "seq"), None),
            P(("grp", "seq"), None),
            P(("grp", "seq")),
            P(("grp", "seq")),
            P(("grp", "seq")),
            P(("grp", "seq")),
            P(("grp", "seq")),
            P(("grp", "seq")),
            P(("grp", "seq")),
            P(("grp", "seq")),
            P(("grp", "seq")),
            P("grp", "seq", None),
        ),
        out_specs=(
            P("grp", "seq", None),
            P("grp", "seq", None),
            P("grp", None),
            P("grp", None),
            P("grp", None),
            P("grp", None),
            P("grp", None),
            P("grp", None),
            P("grp"),
            P("grp"),
            P("grp"),
            P("grp"),
            P("grp"),
            P("grp"),
            P("grp"),
            P("grp"),
            P("grp"),
        ),
        check_vma=False,
    )
```

profile of v0, /device:TPU:0, one launch (start us, length us, event | category | flops | bytes accessed | tf_op | source)
XLA Modules:
  0.0 1315.2 jit_solution(8743969012807511607)
XLA Ops:
  16.2 42.3 %all-reduce.17 = (bf16[1024]{0:T(1024)(128)(2,1)S(1)}, bf16[1024]{0:T(1024)(128)(2,1)S(1)}, bf16[1024]{0:T(1024)(128)(2,1)S(1)}, bf16[1024]{0:T(1024)(128)(2,1)S...) all-reduce(bf16[1024]{0:T(1024)(128)(2,1)S(1)} %dynamic-update-slic, ...), channel_id=1, replica_groups=mesh['grp'=8,'seq'=4] {'grp','seq'}, use_global_device_ids=true, to_apply=%add.1 | all-reduce | flops 8192 | bytes 32768
  58.5 11.7 all-gather.10.cloned.1.call-done
  70.2 4.1 add_convert_fusion.4
  74.4 54.2 %all-gather.16.cloned.1.call-done = bf16[1024,1024]{1,0:T(8,128)(2,1)} async-done(((bf16[32,1024]{1,0:T(8,128)(2,1)}), bf16[1024,1024]{1,0:T(8,128)(2,1)}) %all-gather.16.cloned.1.call-update) | async-done | bytes 2097168 | tf_op jit(solution)/shard_map/all_gather | solution.py:137
  128.6 3.8 fusion.70
  134.9 66.0 %all-gather = bf16[32,1,128]{2,1,0:T(2,128)(2,1)S(1)} all-gather(bf16[1,1,128]{2,1,0:T(2,128)(2,1)S(1)} %bitcast.237), channel_id=1, replica_groups=mesh['grp'=8,'seq'=4] {'grp','seq'}, dimensions={0}, use_global_device_ids=true | all-gather | bytes 8448 | tf_op jit(solution)/shard_map/all_gather | solution.py:145
  205.1 63.5 %all-gather.12.cloned.1.call-done = bf16[4,512,1024]{2,1,0:T(8,128)(2,1)} async-done(((bf16[4,128,1024]{2,1,0:T(8,128)(2,1)}), bf16[4,512,1024]{2,1,0:T(8,128)(2,1)}) %all-gather.12.cloned.1.call-update) | async-done | bytes 4194320 | tf_op jit(solution)/shard_map/all_gather | solution.py:178
  268.6 6.2 copy.51
  274.8 75.1 %all-gather.18.cloned.1.call-done = bf16[4,512,1024]{2,1,0:T(8,128)(2,1)} async-done(((bf16[4,128,1024]{2,1,0:T(8,128)(2,1)}), bf16[4,512,1024]{2,1,0:T(8,128)(2,1)}) %all-gather.18.cloned.1.call-update) | async-done | bytes 4194320 | tf_op jit(solution)/shard_map/all_gather | solution.py:177
  349.9 6.2 copy.53
  356.3 22.6 %while.26 = (s32[]{:T(128)}, bf16[4,128,1024]{1,2,0:T(8,128)(2,1)S(1)}, f32[4,16,128,1]{2,1,3,0:T(8,128)S(1)}, bf16[4,512,1024]{1,2,0:T(8,128)(2,1)}, pred[4,128...) while((s32[]{:T(128)}, ...), condition=%wide.region_3.4_spmd, body=%wide.region_0.3_spmd.sunk | while | flops 281147392 | bytes 20840552 | solution.py:185
  378.9 28.9 %all-gather.20.cloned.1.call-done = bf16[1024,1024]{1,0:T(8,128)(2,1)} async-done(((bf16[32,1024]{1,0:T(8,128)(2,1)}), bf16[1024,1024]{1,0:T(8,128)(2,1)}) %all-gather.20.cloned.1.call-update) | async-done | bytes 2097168 | tf_op jit(solution)/shard_map/all_gather | solution.py:139
  407.7 3.5 fusion.85
  411.6 75.3 %all-gather.22.cloned.1.call-done = bf16[1024,4096]{1,0:T(8,128)(2,1)} async-done(((bf16[32,4096]{1,0:T(8,128)(2,1)}), bf16[1024,4096]{1,0:T(8,128)(2,1)}) %all-gather.22.cloned.1.call-update) | async-done | bytes 8388624 | tf_op jit(solution)/shard_map/all_gather | solution.py:140
  486.9 9.8 fusion.53
  496.7 3.2 copy-done.4
  499.9 20.4 %multiply_convert_fusion.1 = (bf16[4,128,4096]{2,1,0:T(8,128)(2,1)}, f32[4,128,4096]{2,1,0:T(8,128)}) fusion(f32[4,128,4096]{2,1,0:T(8,128)S(1)} %get-tuple-element.279, f32[4096]{0:T(1024)S(1)} %bitcast.235, u8[128,4096]{1,0:T(8,128)(4,1)S(1)} %get-tuple-element.183, u8[128,4096]{1,0:T(8,128)(4,1)S(1)} %get-tuple-element.182), kind=kLoop, calls=%fused_computation.56 | loop fusion | flops 148897792 | bytes 22036480 | tf_op jit(solution)/shard_map/convert_element_type | solution.py:196
  520.3 45.5 %all-gather.24.cloned.1.call-done = bf16[4096,1024]{1,0:T(8,128)(2,1)} async-done(((bf16[128,1024]{1,0:T(8,128)(2,1)}), bf16[4096,1024]{1,0:T(8,128)(2,1)}) %all-gather.24.cloned.1.call-update) | async-done | bytes 8388624 | tf_op jit(solution)/shard_map/all_gather | solution.py:141
  565.9 8.9 fusion.86
  579.7 13.9 %fusion.87 = (bf16[4096]{0:T(1024)(128)(2,1)S(1)}, bf16[4,128,4096]{2,1,0:T(8,128)(2,1)S(1)}) fusion(f32[4,128,4096]{2,1,0:T(8,128)} %get-tuple-element.264, bf16[4,128,1024]{2,1,0:T(8,128)(2,1)S(1)} %get-tuple-element.258, bf16[4096,1024]{1,0:T(8,128)(2,1)} %all-gather.24.cloned.1.call-done, f32[4,128,4096]{2,1,0:T(8,128)} %copy-done.4, ...), kind=kOutput, calls=%fused_computation.141 | convolution fusion | flops 4328517632 | bytes 30433280 | tf_op jit(solution)/shard_map/sce,de->scd/dot_general | solution.py:31
  593.6 10.2 multiply_reduce_fusion.1
  608.9 64.6 %while.27 = (s32[]{:T(128)}, bf16[4,128,1024]{1,2,0:T(8,128)(2,1)}, bf16[4,512,1024]{1,2,0:T(8,128)(2,1)}, bf16[4,512,1024]{1,2,0:T(8,128)(2,1)}, bf16[4,512,102...) while((s32[]{:T(128)}, bf16[4,128,1024]{1,2,0:T(8,128)(2,1)}, ...), condition=%wide.region_14.15_spmd, body=%wide.region_12.14_spmd.sunk | while | flops 688125952 | bytes 65660064 | solution.py:235
  615.4 3.5 multiply_reduce_fusion.6
  631.5 3.5 multiply_reduce_fusion.6
  647.6 3.5 multiply_reduce_fusion.6
  663.8 3.5 multiply_reduce_fusion.6
  673.4 8.2 copy.73
  681.7 6.4 copy.85
  688.2 8.3 copy.75
  696.4 6.4 copy.86
  709.2 54.4 %reduce-scatter.25.cloned.1.call-done = bf16[128,4096]{1,0:T(8,128)(2,1)} async-done(((bf16[512,4096]{1,0:T(8,128)(2,1)}), bf16[128,4096]{1,0:T(8,128)(2,1)}) %reduce-scatter.25.cloned.1.call-update) | async-done | bytes 1048592
  766.5 2.9 fusion.56
  772.0 71.2 %reduce-scatter.27.cloned.1.call-done = bf16[128,4096]{1,0:T(8,128)(2,1)} async-done(((bf16[512,4096]{1,0:T(8,128)(2,1)}), bf16[128,4096]{1,0:T(8,128)(2,1)}) %reduce-scatter.27.cloned.1.call-update) | async-done | bytes 1048592
  852.7 4.4 bitcast_convert_fusion.2
  857.1 9.4 bitcast_convert_fusion.1
  867.8 9.3 bitcast_convert_fusion
  877.2 11.6 reduce-scatter.29.cloned.1.call-done
  890.6 43.0 %reduce-scatter.31.cloned.1.call-done = bf16[128,1024]{1,0:T(8,128)(2,1)} async-done(((bf16[1024,1024]{1,0:T(8,128)(2,1)}), bf16[128,1024]{1,0:T(8,128)(2,1)}) %reduce-scatter.31.cloned.1.call-update) | async-done | bytes 262160
  935.4 42.8 %reduce-scatter.33.cloned.1.call-done = bf16[128,1024]{1,0:T(8,128)(2,1)} async-done(((bf16[1024,1024]{1,0:T(8,128)(2,1)}), bf16[128,1024]{1,0:T(8,128)(2,1)}) %reduce-scatter.33.cloned.1.call-update) | async-done | bytes 262160
  979.9 43.0 %reduce-scatter.19.cloned.1.call-done = bf16[128,1024]{1,0:T(8,128)(2,1)} async-done(((bf16[1024,1024]{1,0:T(8,128)(2,1)}), bf16[128,1024]{1,0:T(8,128)(2,1)}) %reduce-scatter.19.cloned.1.call-update) | async-done | bytes 262160 | tf_op jit(solution)/shard_map/reduce_scatter | solution.py:282
  1022.9 74.6 %reduce-scatter.21.cloned.1.call-done = bf16[128,4096]{1,0:T(8,128)(2,1)} async-done(((bf16[1024,4096]{1,0:T(8,128)(2,1)}), bf16[128,4096]{1,0:T(8,128)(2,1)}) %reduce-scatter.21.cloned.1.call-update) | async-done | bytes 1048592 | tf_op jit(solution)/shard_map/reduce_scatter | solution.py:285
  1097.5 75.0 %reduce-scatter.23.cloned.1.call-done = bf16[512,1024]{1,0:T(8,128)(2,1)} async-done(((bf16[4096,1024]{1,0:T(8,128)(2,1)}), bf16[512,1024]{1,0:T(8,128)(2,1)}) %reduce-scatter.23.cloned.1.call-update) | async-done | bytes 1048592 | tf_op jit(solution)/shard_map/reduce_scatter | solution.py:288
  1174.7 4.2 fusion.44
  1179.4 24.5 %all-reduce.18 = (bf16[1024]{0:T(1024)(128)(2,1)S(1)}, bf16[1024]{0:T(1024)(128)(2,1)S(1)}, bf16[1024]{0:T(1024)(128)(2,1)S(1)}, bf16[4096]{0:T(1024)(128)(2,1)S...) all-reduce(bf16[1024]{0:T(1024)(128)(2,1)S(1)} %reduce_sum.229, ...), channel_id=10, replica_groups=mesh['grp'=8,'seq'=4] {'grp'}, use_global_device_ids=true, to_apply=%region_30.31.clone | all-reduce | flops 12288 | bytes 49152
  1204.5 13.3 %all-reduce.19 = (bf16[128]{0:T(256)(128)(2,1)S(1)}, bf16[128]{0:T(256)(128)(2,1)S(1)}, bf16[128]{0:T(256)(128)(2,1)S(1)}, bf16[512]{0:T(512)(128)(2,1)S(1)}, bf...) all-reduce(bf16[128]{0:T(256)(128)(2,1)S(1)} %dynamic-slice.1, ...), channel_id=1, replica_groups=mesh['grp'=8,'seq'=4] {'seq'}, use_global_device_ids=true, to_apply=%region_31.32 | all-reduce | flops 1536 | bytes 6144 | tf_op jit(solution)/shard_map/psum | solution.py:326
  1222.5 3.2 fusion.40
  1228.3 70.9 %all-reduce.23.cloned.1.call-done = (bf16[128,1024]{0,1:T(8,128)(2,1)}, bf16[128,1024]{0,1:T(8,128)(2,1)}, bf16[128,1024]{0,1:T(8,128)(2,1)}, bf16[128,1024]{1,0...) async-done(((bf16[128,1024]{0,1:T(8,128)(2,1)}, bf16[128,1024]{0,1:T(8,128)(2,1)}, bf16[128,1024]{0,1:T(8,128)(2,1)}, bf16[128,1024]{1,0:T(8,128)(2,1)}, ...) | async-done | bytes 3145744 | tf_op jit(solution)/shard_map/psum | solution.py:320
  1299.2 2.8 convert_element_type.275
  (278 shorter events, 141.7 us)
Async XLA Ops:
  7.2 63.0 %all-gather.10.cloned.1.call-start = ((), (), s32[]{:S(2)}) async-start(), calls=%async_computation.8 | async-start | bytes 2162688 | tf_op jit(solution)/shard_map/all_gather | solution.py:138
  7.9 120.7 %all-gather.16.cloned.1.call-start = ((), (), s32[]{:S(2)}) async-start(), calls=%async_computation.11 | async-start | bytes 2162688 | tf_op jit(solution)/shard_map/all_gather | solution.py:137
  8.7 192.6 %all-gather.14.cloned.1.call-start = ((), (), s32[]{:S(2)}) async-start(), calls=%async_computation.10 | async-start | bytes 2162688 | tf_op jit(solution)/shard_map/all_gather | solution.py:136
  9.4 259.2 %all-gather.12.cloned.1.call-start = ((), (), s32[]{:S(2)}) async-start(), calls=%async_computation.9 | async-start | bytes 5242880 | tf_op jit(solution)/shard_map/all_gather | solution.py:178
  58.5 70.2 %copy-start.14 = (bf16[4,128,1024]{2,1,0:T(8,128)(2,1)S(1)}, bf16[4,128,1024]{2,1,0:T(8,128)(2,1)}, u32[]{:S(2)}) copy-start(bf16[4,128,1024]{2,1,0:T(8,128)(2,1)} %param.22) | copy-start | bytes 3145732
  74.3 60.3 %copy-start.21 = (s32[4,512]{1,0:T(4,128)S(1)}, s32[4,512]{1,0:T(4,128)}, u32[]{:S(2)}) copy-start(s32[4,512]{1,0:T(4,128)} %param.23) | copy-start | bytes 24580
  74.4 60.5 %copy-start.25 = (bf16[128]{0:T(256)(128)(2,1)S(1)}, bf16[128]{0:T(256)(128)(2,1)}, u32[]{:S(2)}) copy-start(bf16[128]{0:T(256)(128)(2,1)} %param.33) | copy-start | bytes 772
  74.4 275.5 %all-gather.18.cloned.1.call-start = ((), (), s32[]{:S(2)}) async-start(), calls=%async_computation.12 | async-start | bytes 5242880 | tf_op jit(solution)/shard_map/all_gather | solution.py:177
  132.5 275.3 %all-gather.20.cloned.1.call-start = ((), (), s32[]{:S(2)}) async-start(), calls=%async_computation.13 | async-start | bytes 2162688 | tf_op jit(solution)/shard_map/all_gather | solution.py:139
  133.1 353.9 %all-gather.22.cloned.1.call-start = ((), (), s32[]{:S(2)}) async-start(), calls=%async_computation.14 | async-start | bytes 8650752 | tf_op jit(solution)/shard_map/all_gather | solution.py:140
  133.8 432.1 %all-gather.24.cloned.1.call-start = ((), (), s32[]{:S(2)}) async-start(), calls=%async_computation.15 | async-start | bytes 8650752 | tf_op jit(solution)/shard_map/all_gather | solution.py:141
  134.6 629.1 %reduce-scatter.25.cloned.1.call-start = ((), (), s32[]{:S(2)}) async-start(), calls=%async_computation.19 | async-start | bytes 5242880
  378.9 28.9 %copy-start.9 = (bf16[4,128,1024]{1,2,0:T(8,128)(2,1)}, bf16[4,128,1024]{1,2,0:T(8,128)(2,1)S(1)}, u32[]{:S(2)}) copy-start(bf16[4,128,1024]{1,2,0:T(8,128)(2,1)S(1)} %get-tuple-element.109) | copy-start | bytes 3145732
  411.3 192.6 %copy-start.1 = (f32[4,128,1024]{2,1,0:T(8,128)}, f32[4,128,1024]{2,1,0:T(8,128)S(1)}, u32[]{:S(2)}) copy-start(f32[4,128,1024]{2,1,0:T(8,128)S(1)} %get-tuple-element.278) | copy-start | bytes 6291460
  496.7 3.2 copy-start.4
  565.9 9.0 copy-start.3
  579.7 13.9 %copy-start.15 = (bf16[4,128,1024]{2,1,0:T(8,128)(2,1)}, bf16[4,128,1024]{2,1,0:T(8,128)(2,1)S(1)}, u32[]{:S(2)}) copy-start(bf16[4,128,1024]{2,1,0:T(8,128)(2,1)S(1)} %get-tuple-element.258) | copy-start | bytes 3145732
  593.6 10.2 copy-start.29
  603.9 1.6 copy-start.10
  604.6 3.2 copy-start.5
  604.8 2.9 copy-start.13
  615.4 3.6 copy-start
  631.5 3.6 copy-start
  647.6 3.6 copy-start
  663.8 3.6 copy-start
  688.1 155.1 %reduce-scatter.27.cloned.1.call-start = ((), (), s32[]{:S(2)}) async-start(), calls=%async_computation.20 | async-start | bytes 5242880
  702.9 185.9 %reduce-scatter.29.cloned.1.call-start = ((), (), s32[]{:S(2)}) async-start(), calls=%async_computation.21 | async-start | bytes 2359296
  709.2 224.4 %reduce-scatter.31.cloned.1.call-start = ((), (), s32[]{:S(2)}) async-start(), calls=%async_computation.22 | async-start | bytes 2359296
  766.5 2.9 copy-start.11
  772.0 206.1 %reduce-scatter.33.cloned.1.call-start = ((), (), s32[]{:S(2)}) async-start(), calls=%async_computation.23 | async-start | bytes 2359296
  852.2 4.9 copy-start.2
  852.2 170.7 %reduce-scatter.19.cloned.1.call-start = ((), (), s32[]{:S(2)}) async-start(), calls=%async_computation.16 | async-start | bytes 2359296 | tf_op jit(solution)/shard_map/reduce_scatter | solution.py:282
  857.1 240.4 %reduce-scatter.21.cloned.1.call-start = ((), (), s32[]{:S(2)}) async-start(), calls=%async_computation.17 | async-start | bytes 9437184 | tf_op jit(solution)/shard_map/reduce_scatter | solution.py:285
  866.6 305.9 %reduce-scatter.23.cloned.1.call-start = ((), (), s32[]{:S(2)}) async-start(), calls=%async_computation.18 | async-start | bytes 9437184 | tf_op jit(solution)/shard_map/reduce_scatter | solution.py:288
  877.1 295.4 %copy-start.27 = (u32[32]{0:T(128)S(1)}, u32[32]{0:T(128)}, u32[]{:S(2)}) copy-start(u32[32]{0:T(128)} %constant.183) | copy-start | bytes 388
  877.1 297.3 %copy-start.8 = (bf16[4,128,1024]{1,2,0:T(8,128)(2,1)S(1)}, bf16[4,128,1024]{1,2,0:T(8,128)(2,1)}, u32[]{:S(2)}) copy-start(bf16[4,128,1024]{1,2,0:T(8,128)(2,1)} %get-tuple-element.111) | copy-start | bytes 3145732
  877.1 422.1 %all-reduce.23.cloned.1.call-start = ((), (), s32[]{:S(2)}) async-start(), calls=%async_computation.24 | async-start | bytes 6291456 | tf_op jit(solution)/shard_map/psum | solution.py:320
  1174.6 4.7 copy-start.22
  1174.6 4.7 copy-start.23
  1174.7 4.7 copy-start.24
  1178.9 46.9 %copy-start.6 = (f32[4,128,1024]{2,1,0:T(8,128)S(1)}, f32[4,128,1024]{2,1,0:T(8,128)}, u32[]{:S(2)}) copy-start(f32[4,128,1024]{2,1,0:T(8,128)} %copy-done.5) | copy-start | bytes 6291460
  1179.4 46.4 %copy-start.12 = (bf16[4,128,1024]{1,2,0:T(8,128)(2,1)S(1)}, bf16[4,128,1024]{1,2,0:T(8,128)(2,1)}, u32[]{:S(2)}) copy-start(bf16[4,128,1024]{1,2,0:T(8,128)(2,1)} %copy.76) | copy-start | bytes 3145732
  1217.8 7.9 copy-start.26
  1217.8 7.9 copy-start.28
  1299.2 5.6 copy-start.20
  1299.2 6.5 copy-start.19
  1299.2 7.4 copy-start.18
  1299.2 8.4 copy-start.17
  (2 other events, 2.4 us)
Sparse Core Ops, SparseCore 0:
  10.9 59.1 all-gather.9
  73.1 55.4 all-gather.15
  131.6 55.3 all-gather.13
  188.9 79.6 all-gather.11
  270.6 79.2 all-gather.17
  352.7 54.9 all-gather.19
  410.7 76.2 all-gather.21
  489.9 75.9 all-gather.23
  688.2 75.3 reduce-scatter.24
  765.9 77.2 reduce-scatter.26
  847.1 41.6 reduce-scatter.28
  892.3 41.2 reduce-scatter.30
  936.8 41.2 reduce-scatter.32
  981.6 41.2 reduce-scatter.18
  1026.2 71.2 reduce-scatter.20
  1101.2 71.2 reduce-scatter.22
  1175.7 123.4 all-reduce.22
where the time goes:
time: 1320 us
  waiting for transfers between devices  845 us (64%)
  blocking collectives  146 us (11%)
  matrix products  146 us (11%)
  local copies, waits for them, and re-layouts  112 us (8%)
  other arithmetic  48.8 us (4%)
  between operations  16.1 us (1%)
    unnamed x22, waiting for transfers between devices  227 us
    all_gather x1, waiting for transfers between devices, local(): lax.all_gather(shards[4], ('grp', 'seq'), axis=0, tiled=True)  75.3 us
    all_gather x1, waiting for transfers between devices, local(): lax.all_gather(own_keys, 'seq', axis=1, tiled=True)  75.1 us
    reduce_scatter x1, waiting for transfers between devices, local(): lax.psum_scatter(gradients[5].astype(jnp.bfloat16), 'grp', scatter_dimens...  75 us
    reduce_scatter x1, waiting for transfers between devices, local(): lax.psum_scatter(gradients[4].astype(jnp.bfloat16), 'grp', scatter_dimens...  74.6 us
    psum x1, waiting for transfers between devices, local(): lax.psum(partial_rows[0].astype(jnp.bfloat16), 'seq').astype(jnp.float32)  70.9 us
    unnamed x2, blocking collectives  66.7 us
    all_gather x1, blocking collectives, local(): lax.all_gather(shards[9], ('grp', 'seq'), axis=0, tiled=True)  66 us
  transfers between devices with their start and end apart: 17, of which 16 were waited for; matrix products, arithmetic and copies ran while one was open for 13% of the time, Pallas kernels for 0%

commit v1 on v0

v1 whole, which is shorter than its diff:
```python
import functools
import math

import jax
import jax.numpy as jnp
from jax import lax
from jax.experimental import pallas as pl
from jax.experimental.pallas import tpu as pltpu
from jax.sharding import PartitionSpec as P

H = 16
HD = 64
LINE = 4
RING = 8
UNITS = 12
MESH = pl.DeviceIdType.MESH
BF = jnp.bfloat16
F32 = jnp.float32
ANY = pl.BlockSpec(memory_space=pl.ANY)


class Place:
    def __init__(self):
        self.g = lax.axis_index("grp")
        self.s = lax.axis_index("seq")
        self.lo = lax.rem(self.g, RING)
        self.c = lax.rem(self.lo, 2)
        xb = lax.rem(self.lo // 2, 2)
        yb = self.lo // 4
        self.dc, self.dx, self.dy = 1 - 2 * self.c, 2 - 4 * xb, 4 - 8 * yb
        self.at_c = (self.g + self.dc, self.s)
        self.at_x = (self.g + self.dx, self.s)
        self.at_y = (self.g + self.dy, self.s)
        self.chip = self.lo // 2
        self.chip_x = self.chip + 1 - 2 * xb
        self.chip_y = self.chip + 2 - 4 * yb
        self.chip_d = self.chip_x + 2 - 4 * yb

    def along(self, t):
        return (self.g, t)


def send(src, dst, send_sem, recv_sem, to):
    return pltpu.make_async_remote_copy(
        src_ref=src, dst_ref=dst, send_sem=send_sem, recv_sem=recv_sem, device_id=to, device_id_type=MESH
    )


def greet(me):
    barrier = pltpu.get_barrier_semaphore()

    def signal(to):
        pl.semaphore_signal(barrier, inc=1, device_id=to, device_id_type=MESH)

    for to in (me.at_c, me.at_x, me.at_y):
        signal(to)
    for t in range(LINE):
        pl.when(me.s != t)(lambda t=t: signal(me.along(t)))
    pl.semaphore_wait(barrier, 3 + LINE - 1)


def exchange_sequences(me, whole, split, sems, index):
    send_sem, recv_sem, local_sem = sems
    block = split.shape[1]

    def copy(t):
        return send(
            split.at[t], whole.at[pl.ds(me.s * block, block)], send_sem.at[index, t], recv_sem.at[index, me.s], me.along(t)
        )

    def landed(t):
        return send(
            split.at[t], whole.at[pl.ds(t * block, block)], send_sem.at[index, t], recv_sem.at[index, t], me.along(t)
        )

    own = pltpu.make_async_copy(split.at[me.s], whole.at[pl.ds(me.s * block, block)], local_sem.at[index])

    def start():
        own.start()
        for t in range(LINE):
            pl.when(me.s != t)(lambda t=t: copy(t).start())

    def wait():
        own.wait()
        for t in range(LINE):
            pl.when(me.s != t)(lambda t=t: landed(t).wait_recv())

    def sent():
        for t in range(LINE):
            pl.when(me.s != t)(lambda t=t: copy(t).wait_send())

    return start, wait, sent


def return_sequences(me, whole, split, sems, index):
    send_sem, recv_sem, local_sem = sems
    block = split.shape[1]

    def copy(t):
        return send(
            whole.at[pl.ds(t * block, block)], split.at[me.s], send_sem.at[index, t], recv_sem.at[index, me.s], me.along(t)
        )

    def landed(t):
        return send(
            whole.at[pl.ds(t * block, block)], split.at[t], send_sem.at[index, t], recv_sem.at[index, t], me.along(t)
        )

    own = pltpu.make_async_copy(whole.at[pl.ds(me.s * block, block)], split.at[me.s], local_sem.at[index])

    def start():
        own.start()
        for t in range(LINE):
            pl.when(me.s != t)(lambda t=t: copy(t).start())

    def wait():
        own.wait()
        for t in range(LINE):
            pl.when(me.s != t)(lambda t=t: landed(t).wait_recv())

    def sent():
        for t in range(LINE):
            pl.when(me.s != t)(lambda t=t: copy(t).wait_send())

    return start, wait, sent


class Gather:
    def __init__(self, me, src, dst, rows, sems, u):
        self.me, self.src, self.dst, self.rows, self.u = me, src, dst, rows, u
        self.local, self.zs, self.zr, self.xs, self.xr, self.cs, self.cr = sems

    def own(self):
        me = self.me
        return pltpu.make_async_copy(self.src, self.dst((me.lo * LINE + me.s) * self.rows, self.rows), self.local.at[self.u])

    def z_copy(self, source, to, slot):
        me = self.me
        there = self.dst((me.lo * LINE + source) * self.rows, self.rows)
        return there, self.zs.at[self.u, slot], self.zr.at[self.u, source], me.along(to)

    def z_direct(self, to):
        me = self.me
        there, ss, rs, dev = self.z_copy(me.s, to, to)
        return send(self.src, there, ss, rs, dev)

    def z_pass(self, source, to):
        there, ss, rs, dev = self.z_copy(source, to, LINE - 1 - source if False else self.pass_slot(to))
        return send(there, there, ss, rs, dev)

    @staticmethod
    def pass_slot(to):
        return 1 if to == 0 else 2

    def start(self):
        me = self.me
        self.own().start()
        for t in range(LINE):
            near = (me.s != t) & (me.s - t <= 2) & (t - me.s <= 2)
            pl.when(near)(lambda t=t: self.z_direct(t).start())

    def z_recv(self, source):
        there, ss, rs, dev = self.z_copy(source, source, source)
        send(there, there, ss, rs, dev).wait_recv()

    def relay(self):
        me = self.me

        @pl.when(me.s == 1)
        def _():
            self.z_recv(3)
            self.z_pass(3, 0).start()

        @pl.when(me.s == 2)
        def _():
            self.z_recv(0)
            self.z_pass(0, 3).start()

    def line_done(self):
        me = self.me
        self.own().wait()
        for t in range(LINE):
            done = (me.s == 1) if t == 3 else ((me.s == 2) if t == 0 else (me.s == LINE))
            pl.when((me.s != t) & jnp.logical_not(done))(lambda t=t: self.z_recv(t))

    def block(self, lo, half=None):
        rows = self.rows * LINE
        if half is None:
            return self.dst(lo * rows, rows)
        return self.dst(lo * rows + half * (rows // 2), rows // 2)

    def x1(self, lo):
        return send(self.block(lo), self.block(lo), self.xs.at[self.u, 0], self.xr.at[self.u, 0], self.me.at_x)

    def y1(self, lo):
        return send(self.block(lo), self.block(lo), self.xs.at[self.u, 1], self.xr.at[self.u, 1], self.me.at_y)

    def x2(self, lo):
        return send(self.block(lo, 1), self.block(lo, 1), self.xs.at[self.u, 2], self.xr.at[self.u, 2], self.me.at_x)

    def y2(self, lo):
        return send(self.block(lo, 0), self.block(lo, 0), self.xs.at[self.u, 3], self.xr.at[self.u, 3], self.me.at_y)

    def core(self, lo, k):
        return send(self.block(lo), self.block(lo), self.cs.at[self.u, k], self.cr.at[self.u, k], self.me.at_c)

    def spread(self):
        me = self.me
        self.x1(me.lo).start()
        self.y1(me.lo).start()
        self.core(me.lo, 0).start()

    def cross(self):
        me = self.me
        lo_x, lo_y = me.lo + me.dx, me.lo + me.dy
        self.x1(lo_x).wait_recv()
        self.y2(lo_x).start()
        self.core(lo_x, 1).start()
        self.y1(lo_y).wait_recv()
        self.x2(lo_y).start()
        self.core(lo_y, 2).start()

    def corner(self):
        me = self.me
        lo_d = me.lo + me.dx + me.dy
        self.x2(lo_d).wait_recv()
        self.y2(lo_d).wait_recv()
        self.core(lo_d, 3).start()

    def whole(self):
        me = self.me
        for k, lo in enumerate((me.lo, me.lo + me.dx, me.lo + me.dy, me.lo + me.dx + me.dy)):
            self.core(lo + me.dc, k).wait_recv()

    def sent(self):
        me = self.me
        for t in range(LINE):
            near = (me.s != t) & (me.s - t <= 2) & (t - me.s <= 2)
            pl.when(near)(lambda t=t: self.z_direct(t).wait_send())
        pl.when(me.s == 1)(lambda: self.z_pass(3, 0).wait_send())
        pl.when(me.s == 2)(lambda: self.z_pass(0, 3).wait_send())
        self.x1(me.lo).wait_send()
        self.y1(me.lo).wait_send()
        self.x2(me.lo + me.dy).wait_send()
        self.y2(me.lo + me.dx).wait_send()
        for k, lo in enumerate((me.lo, me.lo + me.dx, me.lo + me.dy, me.lo + me.dx + me.dy)):
            self.core(lo, k).wait_send()


def rows_of(ref, columns=None):
    if columns is None:
        return lambda row, n: ref.at[pl.ds(row, n)]
    return lambda row, n: ref.at[pl.ds(row, n), columns]


def gather_kernel(
    tok, cot, vec, wq, wk, wv, wo, wi, wu,
    tok_all, cot_all, vec_all, wq_all, wk_all, wv_all, wo_all, wi_all, wu_all,
    local, zs, zr, xs, xr, cs, cr, a_send, a_recv, a_local,
):
    me = Place()
    sems = (local, zs, zr, xs, xr, cs, cr)
    a_sems = (a_send, a_recv, a_local)
    units = [Gather(me, vec, rows_of(vec_all), vec.shape[0], sems, 0)]

    def add(src, ref, columns=None):
        units.append(Gather(me, src, rows_of(ref, columns), src.shape[0], sems, len(units)))

    for src, ref in ((wq, wq_all), (wk, wk_all), (wv, wv_all), (wo, wo_all)):
        add(src, ref)
    width = wi.shape[1] // 4
    for j in range(4):
        add(wi.at[:, pl.ds(j * width, width)], wi_all, pl.ds(j * width, width))
    width = wu.shape[1] // 4
    for j in range(4):
        add(wu.at[:, pl.ds(j * width, width)], wu_all, pl.ds(j * width, width))
    n = len(units)
    greet(me)
    tokens = exchange_sequences(me, tok_all, tok, a_sems, 0)
    seed = exchange_sequences(me, cot_all, cot, a_sems, 1)
    units[0].start()
    units[1].start()
    units[2].start()
    tokens[0]()
    for k in range(n + 3):
        if k < n:
            units[k].relay()
            units[k].line_done()
            units[k].spread()
        if 0 <= k - 1 < n:
            units[k - 1].cross()
        if 0 <= k - 2 < n:
            units[k - 2].corner()
        if 0 <= k - 3 < n:
            units[k - 3].whole()
        if k + 3 < n:
            units[k + 3].start()
        if k == 6:
            seed[0]()
    tokens[1]()
    seed[1]()
    for unit in units:
        unit.sent()
    tokens[2]()
    seed[2]()


def gather_all(tok, cot, vec, weights):
    block = tok.shape[1] * LINE
    outs = [
        jax.ShapeDtypeStruct((block, tok.shape[2]), BF),
        jax.ShapeDtypeStruct((block, tok.shape[2]), BF),
        jax.ShapeDtypeStruct((vec.shape[0] * RING * LINE, vec.shape[1]), BF),
    ] + [jax.ShapeDtypeStruct((w.shape[0] * RING * LINE, w.shape[1]), BF) for w in weights]
    n = UNITS + 1
    dma = pltpu.SemaphoreType.DMA
    return pl.pallas_call(
        gather_kernel,
        out_shape=outs,
        in_specs=[ANY] * 9,
        out_specs=[ANY] * 9,
        scratch_shapes=[
            dma((n,)), dma((n, 4)), dma((n, 4)), dma((n, 4)), dma((n, 4)), dma((n, 4)), dma((n, 4)),
            dma((2, 4)), dma((2, 4)), dma((2,)),
        ],
        compiler_params=pltpu.CompilerParams(collective_id=0, has_side_effects=True, vmem_limit_bytes=56 << 20),
        name="gather_weights",
    )(tok, cot, vec, *weights)


def reduce_kernel(
    gq, gk, gv, go, gi, gu, vec, lay, gtok,
    lay_out, gtok_out, oq, ok, ov, oo, oi, ou, vec_out,
    from_core, half, plane, line, own, acc, zsum, ztot, vbuf, vrecv,
    cs, cr, hs, hr, ps, pr, zs, zr, own_sem, out_sem, vs, vr, vl, a_send, a_recv, a_local,
):
    me = Place()
    a_sems = (a_send, a_recv, a_local)
    rows = oq.shape[0]
    width = oq.shape[1]

    def square(ref, out):
        return (lambda lo: ref.at[pl.ds(lo * rows, rows)], out)

    units = []
    for j in range(4):
        units.append(
            (
                lambda lo, j=j: gu.at[pl.ds(lo * (4 * rows) + j * rows, rows)],
                ou.at[pl.ds(j * rows, rows)],
            )
        )
    for j in range(4):
        columns = pl.ds(j * width, width)
        units.append((lambda lo, columns=columns: gi.at[pl.ds(lo * rows, rows), columns], oi.at[:, columns]))
    units += [square(go, oo), square(gv, ov), square(gk, ok), square(gq, oq)]
    n = len(units)
    slots = acc.shape[0]

    def to_core(u, j):
        return send(units[u][0](2 * j + 1 - me.c), from_core.at[u, j], cs.at[u], cr.at[u], me.at_c)

    def own_load(u, j):
        return pltpu.make_async_copy(units[u][0](2 * j + me.c), own.at[u % slots, j], own_sem.at[u % slots, j])

    def half_x(u):
        a = acc.at[u % slots, me.chip_d, pl.ds(0, rows // 2)]
        return send(a, half.at[u, 0], hs.at[u, 0], hr.at[u, 0], me.at_x)

    def half_y(u):
        a = acc.at[u % slots, me.chip_d, pl.ds(rows // 2, rows // 2)]
        return send(a, half.at[u, 1], hs.at[u, 1], hr.at[u, 1], me.at_y)

    def plane_x(u):
        return send(acc.at[u % slots, me.chip_x], plane.at[u, 0], ps.at[u, 0], pr.at[u, 0], me.at_x)

    def plane_y(u):
        return send(acc.at[u % slots, me.chip_y], plane.at[u, 1], ps.at[u, 1], pr.at[u, 1], me.at_y)

    end = (me.s == 0) | (me.s == 3)
    mid = (me.s == 1) | (me.s == 2)
    partner = me.along(me.s + 1 - 2 * lax.rem(me.s, 2))
    other = me.along(3 - me.s)

    def line_in(u):
        return send(zsum.at[u], line.at[u, 0], zs.at[u, 0], zr.at[u, 0], partner)

    def line_swap(u):
        return send(zsum.at[u], line.at[u, 1], zs.at[u, 0], zr.at[u, 1], other)

    def line_out(u):
        return send(ztot.at[u], line.at[u, 0], zs.at[u, 1], zr.at[u, 0], partner)

    def out_mid(u):
        return pltpu.make_async_copy(ztot.at[u], units[u][1], out_sem.at[u])

    def out_end(u):
        return pltpu.make_async_copy(line.at[u, 0], units[u][1], out_sem.at[u])

    def wide(x):
        return x.astype(F32)

    def s0(u):
        for j in range(4):
            to_core(u, j).start()
        for j in range(4):
            own_load(u, j).start()

    def s1(u):
        if u >= slots:
            sent_acc(u - slots)
        for j in range(4):
            own_load(u, j).wait()
        send(from_core.at[u], from_core.at[u], cs.at[u], cr.at[u], me.at_c).wait_recv()
        slot = u % slots
        acc[slot] = (wide(own[slot]) + wide(from_core[u])).astype(BF)
        half_x(u).start()
        half_y(u).start()

    def s2(u):
        slot = u % slots
        low, high = pl.ds(0, rows // 2), pl.ds(rows // 2, rows // 2)
        half_x(u).wait_recv()
        acc[slot, me.chip_y, low] = (wide(acc[slot, me.chip_y, low]) + wide(half[u, 0])).astype(BF)
        plane_y(u).start()
        half_y(u).wait_recv()
        acc[slot, me.chip_x, high] = (wide(acc[slot, me.chip_x, high]) + wide(half[u, 1])).astype(BF)
        plane_x(u).start()

    def s3(u):
        slot = u % slots
        plane_x(u).wait_recv()
        plane_y(u).wait_recv()
        zsum[u] = (wide(acc[slot, me.chip]) + wide(plane[u, 0]) + wide(plane[u, 1])).astype(BF)
        pl.when(end)(lambda: line_in(u).start())

    def z1(u):
        @pl.when(mid)
        def _():
            line_in(u).wait_recv()
            zsum[u] = (wide(zsum[u]) + wide(line[u, 0])).astype(BF)
            line_swap(u).start()

    def z2(u):
        @pl.when(mid)
        def _():
            line_swap(u).wait_recv()
            ztot[u] = (wide(zsum[u]) + wide(line[u, 1])).astype(BF)
            line_out(u).start()
            out_mid(u).start()

    def z3(u):
        @pl.when(end)
        def _():
            line_out(u).wait_recv()
            out_end(u).start()

    def sent_acc(u):
        half_x(u).wait_send()
        half_y(u).wait_send()
        plane_x(u).wait_send()
        plane_y(u).wait_send()

    def finish(u):
        send(from_core.at[u], from_core.at[u], cs.at[u], cr.at[u], me.at_c).wait_send()
        pl.when(end)(lambda: line_in(u).wait_send())
        pl.when(end)(lambda: out_end(u).wait())

        @pl.when(mid)
        def _():
            line_swap(u).wait_send()
            line_out(u).wait_send()
            out_mid(u).wait()

    def v_swap(k, to):
        return send(vbuf.at[k], vrecv.at[k], vs.at[k], vr.at[k], to)

    v_to = (me.at_c, me.at_x, me.at_y)

    def v_step(k):
        if k == 0:
            pltpu.make_async_copy(vec, vbuf.at[0], vl).start()
            pltpu.make_async_copy(vec, vbuf.at[0], vl).wait()
            v_swap(0, v_to[0]).start()
        elif k < 4:
            v_swap(k - 1, v_to[k - 1]).wait_recv()
            vbuf[k] = vbuf[k - 1] + vrecv[k - 1]
            if k < 3:
                v_swap(k, v_to[k]).start()
            else:
                pl.when(end)(lambda: v_swap(3, partner).start())
        elif k == 4:

            @pl.when(mid)
            def _():
                v_swap(3, partner).wait_recv()
                vbuf[4] = vbuf[3] + vrecv[3]
                v_swap(4, other).start()

        elif k == 5:

            @pl.when(mid)
            def _():
                v_swap(4, other).wait_recv()
                vbuf[5] = vbuf[4] + vrecv[4]
                v_swap(5, partner).start()
                vec_out[...] = vbuf[5]

        elif k == 6:

            @pl.when(end)
            def _():
                v_swap(5, partner).wait_recv()
                vec_out[...] = vrecv[5]

    def v_finish():
        for k in range(3):
            v_swap(k, v_to[k]).wait_send()
        pl.when(end)(lambda: v_swap(3, partner).wait_send())

        @pl.when(mid)
        def _():
            v_swap(4, other).wait_send()
            v_swap(5, partner).wait_send()

    greet(me)
    back = return_sequences(me, lay, lay_out, a_sems, 0)
    back2 = return_sequences(me, gtok, gtok_out, a_sems, 1)
    stages = (s0, s1, s2, s3, z1, z2, z3)
    for k in range(n + len(stages) - 1):
        for d, stage in enumerate(stages):
            if 0 <= k - d < n:
                stage(k - d)
        if k < 7:
            v_step(k)
        if k == 1:
            back[0]()
        if k == 5:
            back2[0]()
    for u in range(n - slots, n):
        sent_acc(u)
    for u in range(n):
        finish(u)
    v_finish()
    back[1]()
    back2[1]()
    back[2]()
    back2[2]()


def reduce_all(grads, vec, lay, gtok, line_block):
    d = grads[0].shape[0]
    rows = d // RING
    n = UNITS
    slots = 4
    dma = pltpu.SemaphoreType.DMA
    vm = pltpu.VMEM
    sq = jax.ShapeDtypeStruct((rows, d), BF)
    outs = [jax.ShapeDtypeStruct((LINE, line_block, d), BF)] * 2 + [
        sq, sq, sq, sq,
        jax.ShapeDtypeStruct((rows, 4 * d), BF),
        jax.ShapeDtypeStruct((4 * rows, d), BF),
        jax.ShapeDtypeStruct(vec.shape, F32),
    ]
    return pl.pallas_call(
        reduce_kernel,
        out_shape=outs,
        in_specs=[ANY] * 9,
        out_specs=[ANY] * 8 + [pl.BlockSpec(memory_space=pltpu.VMEM)],
        scratch_shapes=[
            vm((n, 4, rows, d), BF), vm((n, 2, rows // 2, d), BF), vm((n, 2, rows, d), BF), vm((n, 2, rows, d), BF),
            vm((slots, 4, rows, d), BF), vm((slots, 4, rows, d), BF), vm((n, rows, d), BF), vm((n, rows, d), BF),
            vm((6,) + vec.shape, F32), vm((6,) + vec.shape, F32),
            dma((n,)), dma((n,)), dma((n, 2)), dma((n, 2)), dma((n, 2)), dma((n, 2)), dma((n, 2)), dma((n, 2)),
            dma((slots, 4)), dma((n,)), dma((6,)), dma((6,)), dma,
            dma((2, 4)), dma((2, 4)), dma((2,)),
        ],
        compiler_params=pltpu.CompilerParams(collective_id=1, has_side_effects=True, vmem_limit_bytes=58 << 20),
        name="reduce_grads",
    )(*grads, vec, lay, gtok)


def normalize(row_data, gain_row, shift_row):
    centered = row_data - jnp.mean(row_data, axis=-1, keepdims=True)
    variance = jnp.mean(centered * centered, axis=-1, keepdims=True)
    return centered * lax.rsqrt(variance + 1e-06) * gain_row + shift_row


def exact_gelu(values_in):
    return jax.nn.gelu(values_in, approximate=False)


def dot(a, b):
    return jnp.einsum("ab,bc->ac", a, b, preferred_element_type=F32)


def dot_t(a, b):
    return jnp.einsum("ab,cb->ac", a, b, preferred_element_type=F32)


def t_dot(a, b):
    return jnp.einsum("ab,ac->bc", a, b, preferred_element_type=F32)


def total(x):
    return jnp.sum(x.astype(F32), axis=0)


def heads(x):
    return x.reshape(x.shape[0], H, HD)


def layer(tokens, labels, weights, vectors, seed):
    wq, wk, wv, wo, wi, wu = weights
    bq, bv, bo, bi, bu, g1, s1, g2, s2 = vectors
    queries = (dot(tokens, wq) + bq).astype(BF)
    keys = dot(tokens, wk).astype(BF)
    values = (dot(tokens, wv) + bv).astype(BF)
    places = jnp.arange(labels.shape[0])
    marks = jnp.where(labels != 0, labels, -1 - places)
    allowed = marks[:, None] == marks[None, :]
    scale = 1.0 / math.sqrt(HD)
    raw = jnp.einsum("qhd,khd->hqk", heads(queries), heads(keys), preferred_element_type=F32) * scale
    scores = jnp.where(allowed[None], raw, -1e30)
    probs = jax.nn.softmax(scores, axis=-1)
    low = probs.astype(BF)
    context = jnp.einsum("hqk,khd->qhd", low, heads(values), preferred_element_type=F32)
    context = context.reshape(tokens.shape).astype(BF)
    attention = dot(context, wo) + bo
    first, first_pull = jax.vjp(normalize, tokens.astype(F32) + attention, g1, s1)
    first_low = first.astype(BF)
    inner = dot(first_low, wi) + bi
    hidden, gelu_pull = jax.vjp(exact_gelu, inner)
    hidden = hidden.astype(BF)
    second, second_pull = jax.vjp(normalize, first + dot(hidden, wu) + bu, g2, s2)
    layer_out = second.astype(BF)
    grad_second, grad_g2, grad_s2 = second_pull(seed.astype(F32))
    grad_outer = grad_second.astype(BF)
    (grad_inner,) = gelu_pull(dot_t(grad_outer, wu))
    grad_inner = grad_inner.astype(BF)
    grad_first = grad_second + dot_t(grad_inner, wi)
    grad_resid, grad_g1, grad_s1 = first_pull(grad_first)
    grad_attention = grad_resid.astype(BF)
    grad_context = dot_t(grad_attention, wo).astype(BF)
    grad_probs = jnp.einsum("qhd,khd->hqk", heads(grad_context), heads(values), preferred_element_type=F32)
    grad_scores = (probs * (grad_probs - jnp.sum(probs * grad_probs, axis=-1, keepdims=True))).astype(BF)
    gq = jnp.einsum("hqk,khd->qhd", grad_scores, heads(keys), preferred_element_type=F32) * scale
    gk = jnp.einsum("hqk,qhd->khd", grad_scores, heads(queries), preferred_element_type=F32) * scale
    gv = jnp.einsum("hqk,qhd->khd", low, heads(grad_context), preferred_element_type=F32)
    gq, gk, gv = (x.reshape(tokens.shape).astype(BF) for x in (gq, gk, gv))
    grad_tokens = (grad_resid + dot_t(gq, wq) + dot_t(gk, wk) + dot_t(gv, wv)).astype(BF)
    grads = (
        t_dot(tokens, gq), t_dot(tokens, gk), t_dot(tokens, gv), t_dot(context, grad_attention),
        t_dot(first_low, grad_inner), t_dot(hidden, grad_outer),
    )
    sums = (total(gq), total(gv), total(grad_attention), total(grad_inner), total(grad_outer), grad_g1, grad_s1, grad_g2, grad_s2)
    return layer_out, grad_tokens, tuple(g.astype(BF) for g in grads), sums


def local(tokens, labels, *rest):
    weights, vectors, cotangent = rest[:6], rest[6:15], rest[15]
    groups = lax.axis_size("grp") // RING
    g, s = lax.axis_index("grp"), lax.axis_index("seq")
    lo = lax.rem(g, RING)
    if groups > 1:
        def regroup(w):
            full = lax.all_gather(w, ("grp", "seq"), axis=0, tiled=True)
            n = full.shape[0] // (RING * LINE)
            return lax.dynamic_slice_in_dim(full, (lo * LINE + s) * n, n, 0)

        weights = tuple(regroup(w) for w in weights)
        vectors = tuple(regroup(v) for v in vectors)
    piece = vectors[0].shape[0]
    lanes = 128
    packed = [jnp.pad(v, (0, lanes - v.shape[0]))[None] for v in vectors]
    packed = jnp.concatenate(packed + [jnp.zeros((16 - len(vectors), lanes), BF)], axis=0)
    got = gather_all(tokens, cotangent, packed, weights)
    full_tokens, full_seed, full_vec = got[:3]
    full_weights = got[3:]
    full_vec = full_vec.reshape(RING * LINE, 16, lanes)
    full_vectors = [full_vec[:, i, : v.shape[0]].reshape(-1).astype(F32) for i, v in enumerate(vectors)]
    own_labels = lax.dynamic_index_in_dim(labels, s, 0, keepdims=False)
    lay, gtok, grads, sums = layer(full_tokens, own_labels, full_weights, full_vectors, full_seed)
    d = sums[0].shape[0]
    order = [0, 1, 2, 4, 5, 6, 7, 8, 3]
    stacked = jnp.concatenate([sums[i].reshape(-1, d) for i in order] + [jnp.zeros((4, d), F32)], axis=0)
    out = reduce_all(grads, stacked, lay, gtok, tokens.shape[1])
    layer_out, grad_tokens = out[:2]
    mats = [m.astype(F32) for m in out[2:8]]
    vec = out[8]
    flat = [vec[i] for i in range(8)] + [vec[8:12].reshape(-1)]
    back = dict(zip(order, flat))
    flat = [back[i] for i in range(9)]
    if groups > 1:
        same = [[l + RING * h for h in range(groups)] for l in range(RING)]
        eight = [[l + RING * h for l in range(RING)] for h in range(groups)]

        def rejoin(m):
            m = lax.psum(m, "grp", axis_index_groups=same)
            m = lax.all_gather(m, "grp", axis=0, tiled=True, axis_index_groups=eight)
            n = m.shape[0] // (RING * groups)
            return lax.dynamic_slice_in_dim(m, g * n, n, 0)

        mats = [rejoin(m) for m in mats]
        flat = [lax.psum(v, "grp", axis_index_groups=same) for v in flat]
    flat = [lax.dynamic_slice_in_dim(v, g * (v.shape[0] // (RING * groups)), v.shape[0] // (RING * groups), 0) for v in flat]
    return (layer_out, grad_tokens, *mats, *flat)


def solution(mesh):
    both = ("grp", "seq")
    rows = P("grp", "seq", None)
    return jax.shard_map(
        local,
        mesh=mesh,
        in_specs=(rows, P("grp", None)) + (P(both, None),) * 6 + (P(both),) * 9 + (rows,),
        out_specs=(rows, rows) + (P("grp", None),) * 6 + (P("grp"),) * 9,
        check_vma=False,
    )
```

time: 1320 us -> 503 us (0.38)
  waiting for transfers between devices: 845 us -> 0 us
  Pallas kernels: 0 us -> 296 us
  blocking collectives: 146 us -> 0 us
  local copies, waits for them, and re-layouts: 112 us -> 20.9 us
  other arithmetic: 48.8 us -> 29.1 us
  between operations: 16.1 us -> 1.41 us
    all_gather x8 -> x0, waiting for transfers between devices: 354 us -> none  [the longest x1 75.3 us: local(): lax.all_gather(shards[4], ('grp', 'seq'), axis=0, tiled=True)]
    pallas_call x0 -> x2, Pallas kernels: none -> 296 us  [the longest x1 151 us: gather_all(): pl.pallas_call(gather_kernel, out_shape=outs, in_specs=[ANY] * 9, out_spe...]
    unnamed x22 -> x0, waiting for transfers between devices: 227 us -> none
    reduce_scatter x3 -> x0, waiting for transfers between devices: 193 us -> none  [the longest x1 75 us: local(): lax.psum_scatter(gradients[5].astype(jnp.bfloat16), 'grp', scatter_dimens...]
    psum x1 -> x0, waiting for transfers between devices: 70.9 us -> none  [local(): lax.psum(partial_rows[0].astype(jnp.bfloat16), 'seq').astype(jnp.float32)]
    unnamed x2 -> x0, blocking collectives: 66.7 us -> none
    all_gather x1 -> x0, blocking collectives: 66 us -> none  [local(): lax.all_gather(shards[9], ('grp', 'seq'), axis=0, tiled=True)]
    unnamed x101 -> x74, local copies, waits for them, and re-layouts: 65.9 us -> 5.41 us
  transfers between devices with their start and end apart: 17 -> 0, of which waited for: 16 -> 0; matrix products, arithmetic and copies ran while one was open for 13% -> 0% of each run, Pallas kernels for 0% -> 0%
where the time goes in v1:
time: 503 us; the launch traced here: 499 us
  Pallas kernels  296 us (59%)
  matrix products  152 us (30%)
  other arithmetic  29.1 us (6%)
  local copies, waits for them, and re-layouts  20.9 us (4%)
    pallas_call x1, Pallas kernels, gather_all(): pl.pallas_call(gather_kernel, out_shape=outs, in_specs=[ANY] * 9, out_spe...  151 us
    pallas_call x1, Pallas kernels, reduce_all(): pl.pallas_call(reduce_kernel, out_shape=outs, in_specs=[ANY] * 9, out_spe...  145 us
    dot_general x6, matrix products, dot(): return jnp.einsum('ab,bc->ac', a, b, preferred_element_type=F32)  50.5 us
    dot_general x6, matrix products, dot_t(): return jnp.einsum('ab,cb->ac', a, b, preferred_element_type=F32)  31 us
    dot_general x6, matrix products, t_dot(): return jnp.einsum('ab,ac->bc', a, b, preferred_element_type=F32)  28.3 us
    convert_element_type x1, other arithmetic, layer(): (probs * (grad_probs - jnp.sum(probs * grad_probs, axis=-1, keepdims=True...  11.8 us
    dot_general x1, matrix products, layer(): jnp.einsum('qhd,khd->hqk', heads(grad_context), heads(values), preferred_...  10.8 us

profile of v1, /device:TPU:0, one launch (start us, length us, event | category | flops | bytes accessed | tf_op | source)
XLA Modules:
  0.0 498.6 jit_solution(15671347659837046307)
XLA Ops:
  3.4 1.9 concatenate.6.vec
  5.2 150.7 %gather_weights.1 = (bf16[512,1024]{1,0:T(8,128)(2,1)}, bf16[512,1024]{1,0:T(8,128)(2,1)}, bf16[512,128]{1,0:T(8,128)(2,1)}, bf16[1024,1024]{1,0:T(8,128)(2,1)},...) custom-call(bf16[4,128,1024]{2,1,0:T(8,128)(2,1)} %tok.1, ...), custom_call_target="tpu_custom_call" | custom-call | tf_op jit(solution)/shard_map/gather_weights/pallas_call | solution.py:317
  155.9 1.6 fusion.28
  157.6 3.2 add_convert_fusion.4
  160.8 0.7 copy.48
  161.5 3.5 convolution_convert_fusion.7
  165.6 0.8 compare_select_fusion
  166.6 9.6 %fusion.55 = (f32[16,512]{1,0:T(8,128)S(1)}, f32[16,512,512]{1,2,0:T(8,128)}) fusion(pred[512,512]{0,1:T(8,128)(4,1)S(1)} %broadcast_compare_fusion, bf16[512,16,64]{0,2,1:T(8,128)(2,1)S(1)} %bitcast.112, bf16[512,16,64]{0,2,1:T(8,128)(2,1)S(1)} %bitcast.110), kind=kOutput, calls=%fused_computation.136 | convolution fusion | flops 553648640 | bytes 19169280 | tf_op jit(solution)/shard_map/sub | solution.py:625
  176.3 2.8 add_convert_fusion.3
  179.7 8.7 %fusion.22 = bf16[16,64,512]{2,1,0:T(8,128)(2,1)} fusion(bf16[512,16,64]{0,2,1:T(8,128)(2,1)S(1)} %bitcast.118, f32[16,512,512]{1,2,0:T(8,128)} %get-tuple-element.91, f32[16,512]{1,0:T(8,128)S(1)} %get-tuple-element.90), kind=kOutput, calls=%fused_computation.71 | convolution fusion | flops 545783808 | bytes 18907136 | tf_op jit(solution)/shard_map/hqk,khd->qhd/dot_general | solution.py:627
  188.4 3.3 fusion.56
  192.2 1.0 slice_convert_fusion.2
  193.2 27.7 %multiply_convert_fusion.1 = (bf16[512,4096]{1,0:T(8,128)(2,1)}, f32[512,4096]{1,0:T(8,128)}, f32[512,4096]{1,0:T(8,128)}) fusion(f32[4096]{0:T(1024)S(1)} %bitcast.131, bf16[1024,4096]{1,0:T(8,128)(2,1)} %get-tuple-element.42, f32[512,1024]{1,0:T(8,128)S(1)} %get-tuple-element.93, f32[1024]{0:T(1024)S(1)} %reshape.298, f32[1024]{0:T(1024)S(1)} %reshape.297, ...), kind=kOutput, calls=%fused_computation.10 | convolution fusion | flops 4436000768 | bytes 31485952 | tf_op jit(solution)/shard_map/ab,bc->ac/dot_general | solution.py:594
  220.9 10.0 %fusion.57 = (f32[512]{0:T(512)S(1)}, f32[512,1024]{1,0:T(8,128)S(1)}) fusion(f32[1024]{0:T(1024)S(1)} %reshape.300, bf16[512,4096]{1,0:T(8,128)(2,1)} %get-tuple-element.77, bf16[4096,1024]{1,0:T(8,128)(2,1)} %get-tuple-element.43, f32[1024]{0:T(1024)S(1)} %reshape.298, f32[1024]{0:T(1024)S(1)} %reshape.297, f32[512]{0:T(512)S(1)} %fusion.36, ...), kind=kOutput, calls=%fused_computation.138 | convolution fusion | flops 4298636800 | bytes 16795648 | tf_op jit(solution)/shard_map/ab,bc->ac/dot_general | solution.py:594
  231.4 0.8 fusion.18
  232.2 1.9 fusion.52
  234.4 14.4 %convert_reduce_fusion = (f32[4096]{0:T(1024)S(1)}, bf16[512,4096]{1,0:T(8,128)(2,1)S(1)}) fusion(f32[512,4096]{1,0:T(8,128)} %get-tuple-element.78, f32[512,4096]{1,0:T(8,128)} %get-tuple-element.94, f32[4096]{0:T(1024)S(1)} %bitcast.132, bf16[512,1024]{1,0:T(8,128)(2,1)S(1)} %get-tuple-element.70, bf16[4096,1024]{1,0:T(8,128)(2,1)} %get-tuple-element.43), kind=kOutput, calls=%fused_computation.8 | convolution fusion | flops 4330614784 | bytes 30441472 | tf_op jit(solution)/shard_map/ab,cb->ac/dot_general | solution.py:598
  248.8 9.1 %multiply_reduce_fusion.1 = (f32[1024]{0:T(1024)S(1)}, f32[512]{0:T(512)S(1)}, f32[1024]{0:T(1024)S(1)}, f32[512,1024]{1,0:T(8,128)S(1)}) fusion(f32[512,1024]{1,0:T(8,128)S(1)} %copy-done.1, f32[512]{0:T(512)S(1)} %fusion.36, f32[512]{0:T(512)S(1)} %broadcast_multiply_fusion.1, f32[1024]{0:T(1024)S(1)} %reshape.297, ...), kind=kOutput, calls=%fused_computation.45 | convolution fusion | flops 4300207616 | bytes 18894848 | tf_op jit(solution)/shard_map/ab,cb->ac/dot_general | solution.py:598
  257.9 0.7 fusion.51
  258.7 1.3 copy-done.2
  260.2 1.0 copy-done.17
  261.2 2.3 convolution_convert_fusion.6
  263.5 2.3 copy.51
  265.8 10.8 %multiply_reduce_fusion = (f32[16,512]{1,0:T(8,128)S(1)}, f32[16,512,512]{1,2,0:T(8,128)}) fusion(f32[16,512,512]{1,2,0:T(8,128)} %get-tuple-element.91, f32[16,512]{1,0:T(8,128)S(1)} %get-tuple-element.90, bf16[512,16,64]{0,2,1:T(8,128)(2,1)} %bitcast.120, bf16[512,16,64]{0,2,1:T(8,128)(2,1)S(1)} %bitcast.119), kind=kOutput, calls=%fused_computation.2 | convolution fusion | flops 549445632 | bytes 35717120 | tf_op jit(solution)/shard_map/qhd,khd->hqk/dot_general | solution.py:645
  276.5 11.8 %multiply_convert_fusion = bf16[16,512,512]{1,2,0:T(8,128)(2,1)S(1)} fusion(f32[16,512,512]{1,2,0:T(8,128)} %get-tuple-element.99, f32[16,512]{1,0:T(8,128)S(1)} %get-tuple-element.98, f32[16,512,512]{1,2,0:T(8,128)} %get-tuple-element.91, f32[16,512]{1,0:T(8,128)S(1)} %get-tuple-element.90), kind=kLoop, calls=%fused_computation.1 | loop fusion | flops 16777216 | bytes 42008576 | tf_op jit(solution)/shard_map/convert_element_type | solution.py:646
  288.4 1.5 convert_reduce_fusion.5
  290.0 1.3 fusion.58
  291.3 2.6 multiply_convert_fusion.2
  294.0 1.0 copy-done.10
  294.9 1.3 fusion.59
  296.3 8.7 %convert_reduce_fusion.4 = (f32[16,64]{1,0:T(8,128)S(1)}, bf16[16,64,512]{2,1,0:T(8,128)(2,1)S(1)}) fusion(bf16[512,16,64]{0,2,1:T(8,128)(2,1)S(1)} %bitcast.121, f32[16,512,512]{1,2,0:T(8,128)} %get-tuple-element.91, f32[16,512]{1,0:T(8,128)S(1)} %get-tuple-element.90), kind=kOutput, calls=%fused_computation.48 | convolution fusion | flops 546831360 | bytes 18911232 | tf_op jit(solution)/shard_map/hqk,qhd->khd/dot_general | solution.py:649
  305.0 2.6 add_convert_fusion.1.gtok
  307.8 1.3 concatenate.7.vec
  309.1 10.7 %convolution_convert_fusion.gu = bf16[4096,1024]{1,0:T(8,128)(2,1)} fusion(bf16[512,4096]{1,0:T(8,128)(2,1)} %get-tuple-element.77, bf16[512,1024]{1,0:T(8,128)(2,1)} %copy-done.14), kind=kOutput, calls=%fused_computation.28 | convolution fusion | flops 4299161600 | bytes 13631488 | tf_op jit(solution)/shard_map/ab,ac->bc/dot_general | solution.py:602
  319.8 7.2 %convolution_convert_fusion.1.gi = bf16[1024,4096]{1,0:T(8,128)(2,1)} fusion(bf16[512,4096]{1,0:T(8,128)(2,1)S(1)} %copy-done.34, f32[512,1024]{1,0:T(8,128)S(1)} %copy-done.1, f32[1024]{0:T(1024)S(1)} %reshape.298, f32[1024]{0:T(1024)S(1)} %reshape.297, f32[512]{0:T(512)S(1)} %fusion.36, f32[512]{0:T(512)S(1)} %broadcast_multiply_fusion.1), kind=kOutput, calls=%fused_computation.29 | convolution fusion | flops 4301783040 | bytes 14692352 | tf_op jit(solution)/shard_map/ab,ac->bc/dot_general | solution.py:602
  327.0 2.6 convolution_convert_fusion.2.go
  329.6 2.6 convolution_convert_fusion.3.gv
  332.2 2.6 convolution_convert_fusion.4.gk
  334.9 2.6 convolution_convert_fusion.5.gq
  337.5 144.9 %reduce_grads.1 = (bf16[4,128,1024]{2,1,0:T(8,128)(2,1)}, bf16[4,128,1024]{2,1,0:T(8,128)(2,1)}, bf16[128,1024]{1,0:T(8,128)(2,1)}, bf16[128,1024]{1,0:T(8,128)(...) custom-call(bf16[1024,1024]{1,0:T(8,128)(2,1)} %convolution_convert_, ...), custom_call_target="tpu_custom_call" | custom-call | tf_op jit(solution)/shard_map/reduce_grads/pallas_call | solution.py:565
  482.4 2.9 convert_element_type.299
  485.3 2.9 convert_element_type.300
  488.2 0.8 convert_element_type.295
  489.1 0.8 convert_element_type.296
  489.9 0.8 convert_element_type.297
  490.8 0.8 convert_element_type.298
  496.4 1.0 copy.64
  497.4 1.0 copy.65
  (112 shorter events, 11.0 us)
Async XLA Ops:
  161.5 5.1 %copy-start.6 = (bf16[512,1024]{0,1:T(8,128)(2,1)}, bf16[512,1024]{0,1:T(8,128)(2,1)S(1)}, u32[]{:S(2)}) copy-start(bf16[512,1024]{0,1:T(8,128)(2,1)S(1)} %copy.48) | copy-start | bytes 3145732
  165.6 10.6 %copy-start.4 = (bf16[512,1024]{0,1:T(8,128)(2,1)}, bf16[512,1024]{0,1:T(8,128)(2,1)S(1)}, u32[]{:S(2)}) copy-start(bf16[512,1024]{0,1:T(8,128)(2,1)S(1)} %copy.47) | copy-start | bytes 3145732
  166.6 9.7 %copy-start.20 = (bf16[512,1024]{1,0:T(8,128)(2,1)S(1)}, bf16[512,1024]{1,0:T(8,128)(2,1)}, u32[]{:S(2)}) copy-start(bf16[512,1024]{1,0:T(8,128)(2,1)} %get-tuple-element.35) | copy-start | bytes 3145732
  179.7 8.7 %copy-start.12 = (bf16[512,1024]{0,1:T(8,128)(2,1)}, bf16[512,1024]{0,1:T(8,128)(2,1)S(1)}, u32[]{:S(2)}) copy-start(bf16[512,1024]{0,1:T(8,128)(2,1)S(1)} %copy.49) | copy-start | bytes 3145732
  191.7 29.1 %copy-start = (f32[512,1024]{1,0:T(8,128)}, f32[512,1024]{1,0:T(8,128)S(1)}, u32[]{:S(2)}) copy-start(f32[512,1024]{1,0:T(8,128)S(1)} %get-tuple-element.93) | copy-start | bytes 6291460
  220.9 10.4 %copy-start.8 = (bf16[512,1024]{1,0:T(8,128)(2,1)S(1)}, bf16[512,1024]{1,0:T(8,128)(2,1)}, u32[]{:S(2)}) copy-start(bf16[512,1024]{1,0:T(8,128)(2,1)} %get-tuple-element.39) | copy-start | bytes 3145732
  234.4 14.4 %copy-start.14 = (bf16[512,1024]{1,0:T(8,128)(2,1)}, bf16[512,1024]{1,0:T(8,128)(2,1)S(1)}, u32[]{:S(2)}) copy-start(bf16[512,1024]{1,0:T(8,128)(2,1)S(1)} %get-tuple-element.70) | copy-start | bytes 3145732
  234.4 14.4 %copy-start.1 = (f32[512,1024]{1,0:T(8,128)S(1)}, f32[512,1024]{1,0:T(8,128)}, u32[]{:S(2)}) copy-start(f32[512,1024]{1,0:T(8,128)} %copy-done) | copy-start | bytes 6291460
  248.8 9.1 %copy-start.33 = (bf16[512,4096]{1,0:T(8,128)(2,1)}, bf16[512,4096]{1,0:T(8,128)(2,1)S(1)}, u32[]{:S(2)}) copy-start(bf16[512,4096]{1,0:T(8,128)(2,1)S(1)} %get-tuple-element.68) | copy-start | bytes 12582916
  257.9 3.3 copy-start.9
  258.6 1.3 copy-start.2
  260.2 1.0 copy-start.17
  261.2 4.6 copy-start.13
  276.5 11.9 %copy-start.5 = (bf16[512,1024]{0,1:T(8,128)(2,1)S(1)}, bf16[512,1024]{0,1:T(8,128)(2,1)}, u32[]{:S(2)}) copy-start(bf16[512,1024]{0,1:T(8,128)(2,1)} %copy-done.4) | copy-start | bytes 3145732
  288.4 1.6 copy-start.30
  290.0 1.3 copy-start.7
  291.3 3.6 copy-start.29
  294.0 1.0 copy-start.10
  294.9 1.3 copy-start.19
  296.3 8.7 %copy-start.3 = (f32[512,1024]{1,0:T(8,128)S(1)}, f32[512,1024]{1,0:T(8,128)}, u32[]{:S(2)}) copy-start(f32[512,1024]{1,0:T(8,128)} %copy-done.2) | copy-start | bytes 6291460
  296.3 8.7 %copy-start.28 = (bf16[1024,1024]{1,0:T(8,128)(2,1)S(1)}, bf16[1024,1024]{1,0:T(8,128)(2,1)}, u32[]{:S(2)}) copy-start(bf16[1024,1024]{1,0:T(8,128)(2,1)} %get-tuple-element.40) | copy-start | bytes 6291460
  305.0 2.7 copy-start.31
  309.1 10.7 %copy-start.34 = (bf16[512,4096]{1,0:T(8,128)(2,1)S(1)}, bf16[512,4096]{1,0:T(8,128)(2,1)}, u32[]{:S(2)}) copy-start(bf16[512,4096]{1,0:T(8,128)(2,1)} %copy-done.33) | copy-start | bytes 12582916
  319.8 7.2 %copy-start.18 = (bf16[512,1024]{1,0:T(8,128)(2,1)S(1)}, bf16[512,1024]{1,0:T(8,128)(2,1)}, u32[]{:S(2)}) copy-start(bf16[512,1024]{1,0:T(8,128)(2,1)} %copy-done.17) | copy-start | bytes 3145732
  319.8 7.2 %copy-start.22 = (bf16[16,64,512]{2,1,0:T(8,128)(2,1)S(1)}, bf16[16,64,512]{2,1,0:T(8,128)(2,1)}, u32[]{:S(2)}) copy-start(bf16[16,64,512]{2,1,0:T(8,128)(2,1)} %fusion.22) | copy-start | bytes 3145732
  327.0 2.6 copy-start.21
  327.0 2.6 copy-start.32
  329.6 2.6 copy-start.11
  482.4 5.8 %copy-start.26 = (bf16[128,1024]{1,0:T(8,128)(2,1)S(1)}, bf16[128,1024]{1,0:T(8,128)(2,1)}, u32[]{:S(2)}) copy-start(bf16[128,1024]{1,0:T(8,128)(2,1)} %get-tuple-element.46) | copy-start | bytes 786436
  482.4 6.7 %copy-start.25 = (bf16[128,1024]{1,0:T(8,128)(2,1)S(1)}, bf16[128,1024]{1,0:T(8,128)(2,1)}, u32[]{:S(2)}) copy-start(bf16[128,1024]{1,0:T(8,128)(2,1)} %get-tuple-element.47) | copy-start | bytes 786436
  482.4 7.5 %copy-start.24 = (bf16[128,1024]{1,0:T(8,128)(2,1)S(1)}, bf16[128,1024]{1,0:T(8,128)(2,1)}, u32[]{:S(2)}) copy-start(bf16[128,1024]{1,0:T(8,128)(2,1)} %get-tuple-element.48) | copy-start | bytes 786436
  482.4 8.3 %copy-start.23 = (bf16[128,1024]{1,0:T(8,128)(2,1)S(1)}, bf16[128,1024]{1,0:T(8,128)(2,1)}, u32[]{:S(2)}) copy-start(bf16[128,1024]{1,0:T(8,128)(2,1)} %get-tuple-element.49) | copy-start | bytes 786436
  482.4 9.2 %copy-start.27 = (f32[16,1024]{1,0:T(8,128)S(1)}, f32[16,1024]{1,0:T(8,128)}, u32[]{:S(2)}) copy-start(f32[16,1024]{1,0:T(8,128)} %get-tuple-element.52) | copy-start | bytes 196612
  482.4 14.0 %copy-start.16 = (bf16[4,128,1024]{2,1,0:T(8,128)(2,1)S(1)}, bf16[4,128,1024]{2,1,0:T(8,128)(2,1)}, u32[]{:S(2)}) copy-start(bf16[4,128,1024]{2,1,0:T(8,128)(2,1)} %get-tuple-element.129) | copy-start | bytes 3145732
  485.3 12.0 %copy-start.15 = (bf16[4,128,1024]{2,1,0:T(8,128)(2,1)S(1)}, bf16[4,128,1024]{2,1,0:T(8,128)(2,1)}, u32[]{:S(2)}) copy-start(bf16[4,128,1024]{2,1,0:T(8,128)(2,1)} %get-tuple-element.130) | copy-start | bytes 3145732
